TPU v7x, 32 devices: a whole 2x2x4 slice. The times are simulated.
32 devices in a mesh: seq: 4 (over x, core), ctx: 8 (over z, y).
Axes of the slice: x: 2, y: 2, z: 4, core: 2. Of those that a mesh axis runs over, the one named last changes fastest.
Arguments:
- tokens: bfloat16 [3, 4, 768, 767], P(None, 'seq', 'ctx'), may hold values from -6 to 6
- segment_ids: int32 [3, 4, 768], P(None, 'seq'), may hold values from 0 to 7, never falling along the last dimension, each value on 1 to 576 neighbouring positions
- qkv_weight: bfloat16 [768, 2304], P(('seq', 'ctx')), may hold values from -0.21875 to 0.21875
- out_weight: bfloat16 [768, 767], P(('seq', 'ctx')), may hold values from -0.875 to 0.875
- up_weight: bfloat16 [768, 3072], P(('seq', 'ctx')), may hold values from -0.21875 to 0.21875
- down_weight: bfloat16 [3072, 767], P(('seq', 'ctx')), may hold values from -0.109375 to 0.109375
- attn_gain: bfloat16 [768], P(('seq', 'ctx')), may hold values from 0.099609375 to 1.8984375
- mlp_gain: bfloat16 [768], P(('seq', 'ctx')), may hold values from 0.099609375 to 1.8984375
- out_cotangent: bfloat16 [3, 4, 768, 767], P(None, 'seq', 'ctx'), may hold values from -6 to 6
Outputs:
- result: float32 [3, 4, 768, 767], P(None, 'seq', 'ctx')
- grad_tokens: float32 [3, 4, 768, 767], P(None, 'seq', 'ctx')
- grad_qkv_weight: float32 [768, 2304], P(('seq', 'ctx'))
- grad_out_weight: float32 [768, 767], P(('seq', 'ctx'))
- grad_up_weight: float32 [768, 3072], P(('seq', 'ctx'))
- grad_down_weight: float32 [3072, 767], P(('seq', 'ctx'))
- grad_attn_gain: float32 [768], P(('seq', 'ctx'))
- grad_mlp_gain: float32 [768], P(('seq', 'ctx'))
Inputs may be any that keep to these rules, and one draw needn't show every extreme that they name: `segment_ids`: along each sequence the ids never fall; each of the 8 documents of a sequence has 1 to 576 tokens, and one has exactly 576.
All inputs are finite; a program needn't handle non-finite values.
Results may differ from a plain program's by a relative error of at most 0.014.
Values may be sent and summed in bfloat16 or wider, within the bound.
No kernel may reach another device: no remote copies, remote signals or barrier semaphores. Data moves between devices by JAX's collectives and lax.ppermute only.
A program may use at most 384 MiB of HBM per device.

v0:
```python
import math
import jax
import jax.numpy as jnp
from jax import lax
from jax.sharding import PartitionSpec as P

HEADS = 12
HEAD_DIM = 64
EPS = 1e-05
NEG = -1e30
SCALE = 0.125


def crms(inputs, gains):
    totals = jnp.sum(inputs, axis=-1, keepdims=True)
    meansq = (jnp.sum(inputs * inputs, axis=-1, keepdims=True) + totals * totals) / gains.shape[0]
    return jnp.concatenate([inputs, -totals], axis=-1) * lax.rsqrt(meansq + EPS) * gains


def gelu_tanh(inputs):
    return jax.nn.gelu(inputs, approximate=True)


def matmul(left, right):
    return jnp.dot(left, right, preferred_element_type=jnp.float32)


def matmul_left_t(left, right):
    return lax.dot_general(
        left, right, (((0,), (0,)), ((), ())), preferred_element_type=jnp.float32
    )


def matmul_right_t(left, right):
    return lax.dot_general(
        left, right, (((1,), (1,)), ((), ())), preferred_element_type=jnp.float32
    )


def allowed_pairs(query_pos, query_seg, key_pos, key_seg):
    same_doc = query_seg[:, None, :, None] == key_seg[:, None, None, :]
    causal = query_pos[None, None, :, None] >= key_pos[None, None, None, :]
    return same_doc & causal


def attend_block(state, queries, query_pos, query_seg, keys, values, key_pos, key_seg):
    best, denom, accum = state
    scores = (
        jnp.einsum("bqhd,bkhd->bhqk", queries, keys, preferred_element_type=jnp.float32) * SCALE
    )
    allowed = allowed_pairs(query_pos, query_seg, key_pos, key_seg)
    scores = jnp.where(allowed, scores, NEG)
    peak = jnp.maximum(best, jnp.max(scores, axis=-1))
    weights = jnp.where(allowed, jnp.exp(scores - peak[..., None]), 0.0)
    factor = jnp.exp(best - peak)
    denom = denom * factor + jnp.sum(weights, axis=-1)
    accum = accum * factor[..., None] + jnp.einsum(
        "bhqk,bkhd->bhqd", weights.astype(jnp.bfloat16), values, preferred_element_type=jnp.float32
    )
    return (peak, denom, accum)


def pair_grads(queries, grad_o, lse, delta, query_pos, query_seg, keys, values, key_pos, key_seg):
    scores = (
        jnp.einsum("bqhd,bkhd->bhqk", queries, keys, preferred_element_type=jnp.float32) * SCALE
    )
    allowed = allowed_pairs(query_pos, query_seg, key_pos, key_seg)
    probs = jnp.where(allowed, jnp.exp(scores - lse[..., None]), 0.0)
    dprobs = jnp.einsum("bqhd,bkhd->bhqk", grad_o, values, preferred_element_type=jnp.float32)
    grad_scores = (probs * (dprobs - delta[..., None])).astype(jnp.bfloat16)
    part_q = (
        jnp.einsum("bhqk,bkhd->bqhd", grad_scores, keys, preferred_element_type=jnp.float32) * SCALE
    )
    part_k = (
        jnp.einsum("bhqk,bqhd->bkhd", grad_scores, queries, preferred_element_type=jnp.float32)
        * SCALE
    )
    part_v = jnp.einsum(
        "bhqk,bqhd->bkhd", probs.astype(jnp.bfloat16), grad_o, preferred_element_type=jnp.float32
    )
    return (part_q, part_k, part_v)


def body(
    tokens,
    segment_ids,
    qkv_weight,
    out_weight,
    up_weight,
    down_weight,
    attn_gain,
    mlp_gain,
    out_cotangent,
):
    micro_count, seq_count, local_len, res_width = tokens.shape
    length = segment_ids.shape[2]
    first = lax.axis_index("ctx") * local_len
    query_pos = first + jnp.arange(local_len, dtype=jnp.int32)
    row_count = seq_count * local_len

    def fetch():
        return (
            lax.all_gather(qkv_weight, ("seq", "ctx"), axis=0, tiled=True),
            lax.all_gather(out_weight, ("seq", "ctx"), axis=0, tiled=True),
            lax.all_gather(up_weight, ("seq", "ctx"), axis=0, tiled=True),
            lax.all_gather(down_weight, ("seq", "ctx"), axis=0, tiled=True),
            lax.all_gather(attn_gain, ("seq", "ctx"), axis=0, tiled=True),
            lax.all_gather(mlp_gain, ("seq", "ctx"), axis=0, tiled=True),
        )

    def backward(number, gathered, saved):
        qkv_full, out_full, up_full, down_full, gain_one, gain_two = gathered
        (
            inputs,
            seg_rows,
            query_seg,
            norm_a,
            queries,
            keys_own,
            values_own,
            attn_f32,
            lse,
            attn,
            mixed,
            norm_m,
            pre,
            act,
        ) = saved
        width = qkv_full.shape[0]
        grad_y = out_cotangent[number].reshape(row_count, res_width)
        grad_down = matmul_left_t(act, grad_y)
        grad_act = matmul_right_t(grad_y, down_full)
        _, gelu_pull = jax.vjp(gelu_tanh, pre)
        grad_pre = gelu_pull(grad_act)[0].astype(jnp.bfloat16)
        grad_up = matmul_left_t(norm_m, grad_pre)
        grad_norm_m = matmul_right_t(grad_pre, up_full)
        _, pull_two = jax.vjp(crms, mixed, gain_two.astype(jnp.float32))
        grad_mixed_norm, grad_gain_two = pull_two(grad_norm_m)
        grad_mixed = grad_y.astype(jnp.float32) + grad_mixed_norm
        grad_branch = grad_mixed.astype(jnp.bfloat16)
        grad_outw = matmul_left_t(attn, grad_branch)
        grad_attn = (
            matmul_right_t(grad_branch, out_full)
            .astype(jnp.bfloat16)
            .reshape(seq_count, local_len, HEADS, HEAD_DIM)
        )
        delta = jnp.transpose(jnp.sum(grad_attn.astype(jnp.float32) * attn_f32, axis=-1), (0, 2, 1))
        block_len = math.gcd(length, 1024)
        block_ids = jnp.arange(length // block_len, dtype=jnp.int32)
        keys_all, values_all = (
            lax.all_gather(keys_own, "ctx", axis=1, tiled=True),
            lax.all_gather(values_own, "ctx", axis=1, tiled=True),
        )

        def back_keys(carry, number_block):
            offset = number_block * block_len
            key_block = lax.dynamic_slice_in_dim(keys_all, offset, block_len, 1)
            value_block = lax.dynamic_slice_in_dim(values_all, offset, block_len, 1)
            key_pos = offset + jnp.arange(block_len, dtype=jnp.int32)
            key_seg = lax.dynamic_slice_in_dim(seg_rows, offset, block_len, 1)
            part_q, part_k, part_v = pair_grads(
                queries,
                grad_attn,
                lse,
                delta,
                query_pos,
                query_seg,
                key_block,
                value_block,
                key_pos,
                key_seg,
            )
            return (carry + part_q, jnp.concatenate([part_k, part_v], axis=-1))

        grad_q, terms = lax.scan(back_keys, jnp.zeros(queries.shape, jnp.float32), block_ids)
        terms = jnp.moveaxis(terms, 0, 1).reshape(seq_count, length, HEADS, 2 * HEAD_DIM)
        owned_terms = lax.psum_scatter(terms, "ctx", scatter_dimension=1, tiled=True)
        grad_k = owned_terms[..., :HEAD_DIM]
        grad_v = owned_terms[..., HEAD_DIM:]
        grad_qkv = jnp.concatenate(
            [
                grad_q.reshape(row_count, width),
                grad_k.reshape(row_count, width),
                grad_v.reshape(row_count, width),
            ],
            axis=-1,
        ).astype(jnp.bfloat16)
        grad_qkvw = matmul_left_t(norm_a, grad_qkv)
        grad_norm_a = matmul_right_t(grad_qkv, qkv_full)
        _, pull_one = jax.vjp(crms, inputs, gain_one.astype(jnp.float32))
        grad_input_norm, grad_gain_one = pull_one(grad_norm_a)
        grad_inputs = (grad_mixed + grad_input_norm).reshape(seq_count, local_len, res_width)
        return (
            grad_inputs,
            (grad_qkvw, grad_outw, grad_up, grad_down, grad_gain_one, grad_gain_two),
        )

    outputs = []
    input_grads = []
    owned = None
    for number in range(micro_count):
        (
            forward_qkv_full,
            forward_out_full,
            forward_up_full,
            forward_down_full,
            forward_gain_one,
            forward_gain_two,
        ) = fetch()
        forward_width = forward_qkv_full.shape[0]
        forward_inputs = tokens[number].astype(jnp.float32).reshape(row_count, res_width)
        forward_seg_rows = segment_ids[number]
        forward_query_seg = lax.dynamic_slice_in_dim(forward_seg_rows, first, local_len, 1)
        forward_norm_a = crms(forward_inputs, forward_gain_one.astype(jnp.float32)).astype(
            jnp.bfloat16
        )
        qkv = matmul(forward_norm_a, forward_qkv_full).astype(jnp.bfloat16)
        forward_queries = qkv[:, :forward_width].reshape(seq_count, local_len, HEADS, HEAD_DIM)
        forward_keys_own = qkv[:, forward_width : 2 * forward_width].reshape(
            seq_count, local_len, HEADS, HEAD_DIM
        )
        forward_values_own = qkv[:, 2 * forward_width :].reshape(
            seq_count, local_len, HEADS, HEAD_DIM
        )

        def fold_keys(state, piece):
            keys_part, values_part = piece
            span = keys_part.shape[1]
            block_len = span if span <= 1024 else math.gcd(span, 1024)

            def inner(carry, number_block):
                offset = number_block * block_len
                key_block = lax.dynamic_slice_in_dim(keys_part, offset, block_len, 1)
                value_block = lax.dynamic_slice_in_dim(values_part, offset, block_len, 1)
                key_pos = offset + jnp.arange(block_len, dtype=jnp.int32)
                key_seg = lax.dynamic_slice_in_dim(forward_seg_rows, offset, block_len, 1)
                return (
                    attend_block(
                        carry,
                        forward_queries,
                        query_pos,
                        forward_query_seg,
                        key_block,
                        value_block,
                        key_pos,
                        key_seg,
                    ),
                    None,
                )

            state, _ = lax.scan(inner, state, jnp.arange(span // block_len, dtype=jnp.int32))
            return state

        initial = (
            jnp.full((seq_count, HEADS, local_len), NEG, jnp.float32),
            jnp.zeros((seq_count, HEADS, local_len), jnp.float32),
            jnp.zeros((seq_count, HEADS, local_len, HEAD_DIM), jnp.float32),
        )
        best, denom, accum = fold_keys(
            initial,
            (
                lax.all_gather(forward_keys_own, "ctx", axis=1, tiled=True),
                lax.all_gather(forward_values_own, "ctx", axis=1, tiled=True),
            ),
        )
        heads_out = accum / denom[..., None]
        forward_lse = best + jnp.log(denom)
        forward_attn_f32 = jnp.transpose(heads_out, (0, 2, 1, 3))
        forward_attn = forward_attn_f32.reshape(row_count, forward_width).astype(jnp.bfloat16)
        forward_mixed = forward_inputs + matmul(forward_attn, forward_out_full)
        forward_norm_m = crms(forward_mixed, forward_gain_two.astype(jnp.float32)).astype(
            jnp.bfloat16
        )
        forward_pre = matmul(forward_norm_m, forward_up_full)
        forward_act = gelu_tanh(forward_pre).astype(jnp.bfloat16)
        result = (forward_mixed + matmul(forward_act, forward_down_full)).reshape(
            seq_count, local_len, res_width
        )
        forward_saved = (
            forward_inputs,
            forward_seg_rows,
            forward_query_seg,
            forward_norm_a,
            forward_queries,
            forward_keys_own,
            forward_values_own,
            forward_attn_f32,
            forward_lse,
            forward_attn,
            forward_mixed,
            forward_norm_m,
            forward_pre,
            forward_act,
        )
        result, saved = (result, forward_saved)
        grad_inputs, grads = backward(number, fetch(), saved)
        outputs.append(result)
        input_grads.append(grad_inputs)
        shares = (
            lax.psum_scatter(grads[0], ("seq", "ctx"), scatter_dimension=0, tiled=True),
            lax.psum_scatter(grads[1], ("seq", "ctx"), scatter_dimension=0, tiled=True),
            lax.psum_scatter(grads[2], ("seq", "ctx"), scatter_dimension=0, tiled=True),
            lax.psum_scatter(grads[3], ("seq", "ctx"), scatter_dimension=0, tiled=True),
            lax.psum_scatter(grads[4], ("seq", "ctx"), scatter_dimension=0, tiled=True),
            lax.psum_scatter(grads[5], ("seq", "ctx"), scatter_dimension=0, tiled=True),
        )
        owned = shares if owned is None else jax.tree.map(jnp.add, owned, shares)
    return (jnp.stack(outputs), jnp.stack(input_grads)) + tuple(owned)


def solution(mesh):
    return jax.shard_map(
        body,
        mesh=mesh,
        in_specs=(
            P(None, "seq", "ctx", None),
            P(None, "seq", None),
            P(("seq", "ctx"), None),
            P(("seq", "ctx"), None),
            P(("seq", "ctx"), None),
            P(("seq", "ctx"), None),
            P(("seq", "ctx")),
            P(("seq", "ctx")),
            P(None, "seq", "ctx", None),
        ),
        out_specs=(
            P(None, "seq", "ctx", None),
            P(None, "seq", "ctx", None),
            P(("seq", "ctx"), None),
            P(("seq", "ctx"), None),
            P(("seq", "ctx"), None),
            P(("seq", "ctx"), None),
            P(("seq", "ctx")),
            P(("seq", "ctx")),
        ),
        check_vma=False,
    )
```

profile of v0, /device:TPU:0, one launch (start us, length us, event | category | flops | bytes accessed | tf_op | source)
XLA Modules:
  0.0 1496.1 jit_solution(17649437479589515464)
XLA Ops:
  10.4 42.3 %all-reduce.5 = (bf16[768]{0:T(1024)(128)(2,1)S(1)}, bf16[768]{0:T(1024)(128)(2,1)S(1)}) all-reduce(bf16[768]{0:T(1024)(128)(2,1)S(1)} %dynamic-update-slice, bf16[768]{0:T(1024)(128)(2,1)S(1)} %dynamic-update-slice.1), channel_id=1, replica_groups=mesh['seq'=4,'ctx'=8] {'seq','ctx'}, use_global_device_ids=true, to_apply=%add | all-reduce | flops 1536 | bytes 6144
  53.6 20.3 %all-gather.11.cloned.1.call-done = bf16[768,2304]{1,0:T(8,128)(2,1)} async-done(((bf16[24,2304]{1,0:T(8,128)(2,1)}), bf16[768,2304]{1,0:T(8,128)(2,1)}) %all-gather.11.cloned.1.call-update) | async-done | bytes 3538960 | tf_op jit(solution)/shard_map/all_gather | solution.py:103
  116.3 23.6 %all-gather.27.cloned.1.call-done = bf16[1,768,12,64]{3,2,0,1:T(8,128)(2,1)} async-done(((bf16[1,96,12,64]{3,2,0,1:T(8,128)(2,1)}), bf16[1,768,12,64]{3,2,0,1:T(8,128)(2,1)}) %all-gather.27.cloned.1.call-update) | async-done | bytes 1179664 | tf_op jit(solution)/shard_map/all_gather | solution.py:262
  139.9 4.6 copy.284
  144.5 57.3 %all-gather.29.cloned.1.call-done = bf16[1,768,12,64]{3,2,0,1:T(8,128)(2,1)} async-done(((bf16[1,96,12,64]{3,2,0,1:T(8,128)(2,1)}), bf16[1,768,12,64]{3,2,0,1:T(8,128)(2,1)}) %all-gather.29.cloned.1.call-update) | async-done | bytes 1179664 | tf_op jit(solution)/shard_map/all_gather | solution.py:263
  201.8 4.6 copy.287
  206.4 56.5 %all-gather.23.cloned.1.call-done = bf16[1,768,12,64]{3,2,0,1:T(8,128)(2,1)} async-done(((bf16[1,96,12,64]{3,2,0,1:T(8,128)(2,1)}), bf16[1,768,12,64]{3,2,0,1:T(8,128)(2,1)}) %all-gather.23.cloned.1.call-update) | async-done | bytes 1179664 | tf_op jit(solution)/shard_map/all_gather | solution.py:262
  262.9 4.7 copy.274
  267.6 56.5 %all-gather.25.cloned.1.call-done = bf16[1,768,12,64]{3,2,0,1:T(8,128)(2,1)} async-done(((bf16[1,96,12,64]{3,2,0,1:T(8,128)(2,1)}), bf16[1,768,12,64]{3,2,0,1:T(8,128)(2,1)}) %all-gather.25.cloned.1.call-update) | async-done | bytes 1179664 | tf_op jit(solution)/shard_map/all_gather | solution.py:263
  324.1 4.6 copy.277
  328.6 56.6 %all-gather.13.cloned.1.call-done = bf16[1,768,12,64]{3,2,0,1:T(8,128)(2,1)} async-done(((bf16[1,96,12,64]{3,2,0,1:T(8,128)(2,1)}), bf16[1,768,12,64]{3,2,0,1:T(8,128)(2,1)}) %all-gather.13.cloned.1.call-update) | async-done | bytes 1179664 | tf_op jit(solution)/shard_map/all_gather | solution.py:262
  385.2 4.6 copy.264
  389.8 56.7 %all-gather.15.cloned.1.call-done = bf16[1,768,12,64]{3,2,0,1:T(8,128)(2,1)} async-done(((bf16[1,96,12,64]{3,2,0,1:T(8,128)(2,1)}), bf16[1,768,12,64]{3,2,0,1:T(8,128)(2,1)}) %all-gather.15.cloned.1.call-update) | async-done | bytes 1179664 | tf_op jit(solution)/shard_map/all_gather | solution.py:263
  446.5 4.6 copy.267
  457.8 44.4 %all-gather.17.cloned.1.call-done = bf16[768,767]{1,0:T(8,128)(2,1)} async-done(((bf16[24,767]{1,0:T(8,128)(2,1)}), bf16[768,767]{1,0:T(8,128)(2,1)}) %all-gather.17.cloned.1.call-update) | async-done | bytes 1178128 | tf_op jit(solution)/shard_map/all_gather | solution.py:104
  519.9 47.9 %all-gather.19.cloned.1.call-done = bf16[768,3072]{1,0:T(8,128)(2,1)} async-done(((bf16[24,3072]{1,0:T(8,128)(2,1)}), bf16[768,3072]{1,0:T(8,128)(2,1)}) %all-gather.19.cloned.1.call-update) | async-done | bytes 4718608 | tf_op jit(solution)/shard_map/all_gather | solution.py:105
  572.1 60.9 %all-gather.21.cloned.1.call-done = bf16[3072,767]{1,0:T(8,128)(2,1)} async-done(((bf16[96,767]{1,0:T(8,128)(2,1)}), bf16[3072,767]{1,0:T(8,128)(2,1)}) %all-gather.21.cloned.1.call-update) | async-done | bytes 4712464 | tf_op jit(solution)/shard_map/all_gather | solution.py:106
  633.0 4.9 fusion.128
  653.5 31.2 %while.11 = (s32[]{:T(128)}, f32[1,96,12,64]{1,3,2,0:T(8,128)}, f32[3,1,256,12,128]{4,2,0,3,1:T(8,128)}, s32[3]{0:T(128)S(1)}, bf16[1,768,12,64]{1,3,2,0:T(8,128...) while((s32[]{:T(128)}, f32[1,96,12,64]{1,3,2,0:T(8,128)}, ...), condition=%wide.region_33.34_spmd.clone, body=%wide.region_32.33_spmd.clone.sunk | while | flops 191693152 | bytes 18910308 | solution.py:175
  691.7 31.4 %while.10 = (s32[]{:T(128)}, f32[1,96,12,64]{1,3,2,0:T(8,128)}, f32[3,1,256,12,128]{4,2,0,3,1:T(8,128)}, s32[3]{0:T(128)S(1)}, bf16[1,768,12,64]{1,3,2,0:T(8,128...) while((s32[]{:T(128)}, f32[1,96,12,64]{1,3,2,0:T(8,128)}, ...), condition=%wide.region_27.28_spmd.clone, body=%wide.region_26.27_spmd.clone.sunk | while | flops 191693152 | bytes 18895424 | solution.py:175
  727.9 26.4 %while.9 = (s32[]{:T(128)}, f32[1,96,12,64]{1,3,2,0:T(8,128)}, f32[3,1,256,12,128]{4,2,0,3,1:T(8,128)}, s32[3]{0:T(128)S(1)}, bf16[1,768,12,64]{1,3,2,0:T(8,128)...) while((s32[]{:T(128)}, f32[1,96,12,64]{1,3,2,0:T(8,128)}, ...), condition=%wide.region_21.22_spmd.clone, body=%wide.region_20.21_spmd.clone.sunk | while | flops 191693152 | bytes 18846272 | solution.py:175
  763.3 5.4 add_add_fusion
  773.8 5.0 add_add_fusion.1
  788.8 89.0 %reduce-scatter.10.cloned.1.call-done = f32[1,96,12,128]{3,1,2,0:T(8,128)} async-done(((f32[1,768,12,128]{3,1,2,0:T(8,128)}), f32[1,96,12,128]{3,1,2,0:T(8,128)}) %reduce-scatter.10.cloned.1.call-update) | async-done | bytes 589840 | tf_op jit(solution)/shard_map/reduce_scatter | solution.py:177
  882.3 94.1 %reduce-scatter.8.cloned.1.call-done = f32[1,96,12,128]{3,1,2,0:T(8,128)} async-done(((f32[1,768,12,128]{3,1,2,0:T(8,128)}), f32[1,96,12,128]{3,1,2,0:T(8,128)}) %reduce-scatter.8.cloned.1.call-update) | async-done | bytes 589840 | tf_op jit(solution)/shard_map/reduce_scatter | solution.py:177
  994.2 4.3 fusion.97
  998.6 4.4 fusion.98
  1015.4 40.5 %all-reduce.4 = (f32[768]{0:T(1024)S(1)}, f32[768]{0:T(1024)S(1)}) all-reduce(f32[768]{0:T(1024)S(1)} %add_add_fusion.11, f32[768]{0:T(1024)S(1)} %copy-done.101), channel_id=21, replica_groups=mesh['seq'=4,'ctx'=8] {'seq','ctx'}, use_global_device_ids=true, to_apply=%region_49.50.clone | all-reduce | flops 1536 | bytes 12288
  1057.0 24.0 %reduce-scatter.16.cloned.1.call-done = f32[24,767]{1,0:T(8,128)} async-done(((f32[768,767]{1,0:T(8,128)}), f32[24,767]{1,0:T(8,128)}) %reduce-scatter.16.cloned.1.call-update) | async-done | bytes 73648 | tf_op jit(solution)/shard_map/reduce_scatter | solution.py:301
  1081.0 142.0 %reduce-scatter.20.cloned.1.call-done = f32[96,767]{1,0:T(8,128)} async-done(((f32[3072,767]{1,0:T(8,128)}), f32[96,767]{1,0:T(8,128)}) %reduce-scatter.20.cloned.1.call-update) | async-done | bytes 294544 | tf_op jit(solution)/shard_map/reduce_scatter | solution.py:303
  1223.1 140.9 %reduce-scatter.18.cloned.1.call-done = f32[24,3072]{1,0:T(8,128)} async-done(((f32[768,3072]{1,0:T(8,128)}), f32[24,3072]{1,0:T(8,128)}) %reduce-scatter.18.cloned.1.call-update) | async-done | bytes 294928 | tf_op jit(solution)/shard_map/reduce_scatter | solution.py:302
  1363.9 125.2 %reduce-scatter.14.cloned.1.call-done = f32[24,2304]{1,0:T(8,128)} async-done(((f32[768,2304]{1,0:T(8,128)}), f32[24,2304]{1,0:T(8,128)}) %reduce-scatter.14.cloned.1.call-update) | async-done | bytes 221200 | tf_op jit(solution)/shard_map/reduce_scatter | solution.py:300
  (706 shorter events, 242.1 us)
Async XLA Ops:
  7.2 66.7 %all-gather.11.cloned.1.call-start = ((), (), s32[]{:S(2)}) async-start(), calls=%async_computation.7 | async-start | bytes 3649536 | tf_op jit(solution)/shard_map/all_gather | solution.py:103
  7.9 132.0 %all-gather.27.cloned.1.call-start = ((), (), s32[]{:S(2)}) async-start(), calls=%async_computation.15 | async-start | bytes 3538944 | tf_op jit(solution)/shard_map/all_gather | solution.py:262
  9.9 66.8 %copy-start.20 = (bf16[1,1,96,767]{2,3,1,0:T(8,128)(2,1)}, bf16[1,1,96,767]{2,3,1,0:T(8,128)(2,1)S(1)}, u32[]{:S(2)}) copy-start(bf16[1,1,96,767]{2,3,1,0:T(8,128)(2,1)S(1)} %copy.348) | copy-start | bytes 441796
  52.7 51.6 %copy-start.75 = (f32[768]{0:T(1024)}, f32[768]{0:T(1024)S(1)}, u32[]{:S(2)}) copy-start(f32[768]{0:T(1024)S(1)} %convert_element_type.210) | copy-start | bytes 9220
  80.5 121.3 %all-gather.29.cloned.1.call-start = ((), (), s32[]{:S(2)}) async-start(), calls=%async_computation.16 | async-start | bytes 3538944 | tf_op jit(solution)/shard_map/all_gather | solution.py:263
  84.3 178.6 %all-gather.23.cloned.1.call-start = ((), (), s32[]{:S(2)}) async-start(), calls=%async_computation.13 | async-start | bytes 3538944 | tf_op jit(solution)/shard_map/all_gather | solution.py:262
  95.1 229.0 %all-gather.25.cloned.1.call-start = ((), (), s32[]{:S(2)}) async-start(), calls=%async_computation.14 | async-start | bytes 3538944 | tf_op jit(solution)/shard_map/all_gather | solution.py:263
  98.9 286.3 %all-gather.13.cloned.1.call-start = ((), (), s32[]{:S(2)}) async-start(), calls=%async_computation.8 | async-start | bytes 3538944 | tf_op jit(solution)/shard_map/all_gather | solution.py:262
  106.5 340.0 %all-gather.15.cloned.1.call-start = ((), (), s32[]{:S(2)}) async-start(), calls=%async_computation.9 | async-start | bytes 3538944 | tf_op jit(solution)/shard_map/all_gather | solution.py:263
  107.8 394.4 %all-gather.17.cloned.1.call-start = ((), (), s32[]{:S(2)}) async-start(), calls=%async_computation.10 | async-start | bytes 1216512 | tf_op jit(solution)/shard_map/all_gather | solution.py:104
  108.6 459.2 %all-gather.19.cloned.1.call-start = ((), (), s32[]{:S(2)}) async-start(), calls=%async_computation.11 | async-start | bytes 4866048 | tf_op jit(solution)/shard_map/all_gather | solution.py:105
  109.3 523.7 %all-gather.21.cloned.1.call-start = ((), (), s32[]{:S(2)}) async-start(), calls=%async_computation.12 | async-start | bytes 4866048 | tf_op jit(solution)/shard_map/all_gather | solution.py:106
  109.9 674.3 %reduce-scatter.12.cloned.1.call-start = ((), (), s32[]{:S(2)}) async-start(), calls=%async_computation.19 | async-start | bytes 5308416 | tf_op jit(solution)/shard_map/reduce_scatter | solution.py:177
  457.8 48.7 %copy-start.73 = (bf16[1,96,12,64]{1,3,2,0:T(8,128)(2,1)}, bf16[1,96,12,64]{1,3,2,0:T(8,128)(2,1)S(1)}, u32[]{:S(2)}) copy-start(bf16[1,96,12,64]{1,3,2,0:T(8,128)(2,1)S(1)} %get-tuple-element.733) | copy-start | bytes 442372
  504.1 145.3 %copy-start.6 = (f32[96,767]{0,1:T(8,128)}, f32[96,767]{0,1:T(8,128)S(1)}, u32[]{:S(2)}) copy-start(f32[96,767]{0,1:T(8,128)S(1)} %get-tuple-element.735) | copy-start | bytes 883588
  504.1 63.6 %copy-start.115 = (f32[96,1]{0,1:T(1,128)}, f32[96,1]{0,1:T(1,128)S(1)}, u32[]{:S(2)}) copy-start(f32[96,1]{0,1:T(1,128)S(1)} %bitcast_negate_fusion) | copy-start | bytes 1156
  511.7 134.5 %copy-start.8 = (f32[96,767]{0,1:T(8,128)}, f32[96,767]{0,1:T(8,128)S(1)}, u32[]{:S(2)}) copy-start(f32[96,767]{0,1:T(8,128)S(1)} %get-tuple-element.740) | copy-start | bytes 883588
  511.7 127.7 %copy-start.118 = (f32[96,1]{0,1:T(1,128)}, f32[96,1]{0,1:T(1,128)S(1)}, u32[]{:S(2)}) copy-start(f32[96,1]{0,1:T(1,128)S(1)} %bitcast_negate_fusion.2) | copy-start | bytes 1156
  518.5 53.6 %copy-start.61 = (bf16[1,96,12,64]{1,3,2,0:T(8,128)(2,1)}, bf16[1,96,12,64]{1,3,2,0:T(8,128)(2,1)S(1)}, u32[]{:S(2)}) copy-start(bf16[1,96,12,64]{1,3,2,0:T(8,128)(2,1)S(1)} %get-tuple-element.743) | copy-start | bytes 442372
  519.1 53.0 %copy-start.143 = (f32[96]{0:T(128)}, f32[96]{0:T(128)S(1)}, u32[]{:S(2)}) copy-start(f32[96]{0:T(128)S(1)} %get-tuple-element.580) | copy-start | bytes 1156
  519.1 53.0 %copy-start.145 = (f32[96]{0:T(128)}, f32[96]{0:T(128)S(1)}, u32[]{:S(2)}) copy-start(f32[96]{0:T(128)S(1)} %get-tuple-element.581) | copy-start | bytes 1156
  519.1 127.1 %copy-start.11 = (f32[96,767]{0,1:T(8,128)}, f32[96,767]{0,1:T(8,128)S(1)}, u32[]{:S(2)}) copy-start(f32[96,767]{0,1:T(8,128)S(1)} %get-tuple-element.745) | copy-start | bytes 883588
  519.1 124.4 %copy-start.124 = (f32[96,1]{0,1:T(1,128)}, f32[96,1]{0,1:T(1,128)S(1)}, u32[]{:S(2)}) copy-start(f32[96,1]{0,1:T(1,128)S(1)} %bitcast_negate_fusion.4) | copy-start | bytes 1156
  519.2 53.0 %copy-start.121 = (f32[96]{0:T(128)}, f32[96]{0:T(128)S(1)}, u32[]{:S(2)}) copy-start(f32[96]{0:T(128)S(1)} %fusion.284) | copy-start | bytes 1156
  519.2 127.0 %copy-start.103 = (f32[96]{0:T(128)}, f32[96]{0:T(128)S(1)}, u32[]{:S(2)}) copy-start(f32[96]{0:T(128)S(1)} %fusion.282) | copy-start | bytes 1156
  519.2 127.0 %copy-start.105 = (f32[96]{0:T(128)}, f32[96]{0:T(128)S(1)}, u32[]{:S(2)}) copy-start(f32[96]{0:T(128)S(1)} %fusion.280) | copy-start | bytes 1156
  684.8 192.9 %reduce-scatter.10.cloned.1.call-start = ((), (), s32[]{:S(2)}) async-start(), calls=%async_computation.18 | async-start | bytes 5308416 | tf_op jit(solution)/shard_map/reduce_scatter | solution.py:177
  723.1 253.3 %reduce-scatter.8.cloned.1.call-start = ((), (), s32[]{:S(2)}) async-start(), calls=%async_computation.17 | async-start | bytes 5308416 | tf_op jit(solution)/shard_map/reduce_scatter | solution.py:177
  754.4 326.7 %reduce-scatter.16.cloned.1.call-start = ((), (), s32[]{:S(2)}) async-start(), calls=%async_computation.21 | async-start | bytes 2433024 | tf_op jit(solution)/shard_map/reduce_scatter | solution.py:301
  759.0 464.0 %reduce-scatter.20.cloned.1.call-start = ((), (), s32[]{:S(2)}) async-start(), calls=%async_computation.23 | async-start | bytes 9732096 | tf_op jit(solution)/shard_map/reduce_scatter | solution.py:303
  768.8 595.2 %reduce-scatter.18.cloned.1.call-start = ((), (), s32[]{:S(2)}) async-start(), calls=%async_computation.22 | async-start | bytes 9732096 | tf_op jit(solution)/shard_map/reduce_scatter | solution.py:302
  778.8 710.3 %reduce-scatter.14.cloned.1.call-start = ((), (), s32[]{:S(2)}) async-start(), calls=%async_computation.20 | async-start | bytes 7299072 | tf_op jit(solution)/shard_map/reduce_scatter | solution.py:300
  (180 other events, 501.8 us)
Sparse Core Ops, SparseCore 0:
  10.9 62.9 all-gather.10
  80.6 59.2 all-gather.26
  142.7 59.0 all-gather.28
  203.8 59.0 all-gather.22
  265.0 59.0 all-gather.24
  326.1 59.0 all-gather.12
  387.4 59.0 all-gather.14
  449.4 52.7 all-gather.16
  505.2 62.5 all-gather.18
  570.5 62.4 all-gather.20
  684.9 94.0 reduce-scatter.11
  782.5 95.1 reduce-scatter.9
  881.4 94.9 reduce-scatter.7
  982.1 98.8 reduce-scatter.15
  1088.4 134.6 reduce-scatter.19
  1229.4 134.4 reduce-scatter.17
  1371.0 118.1 reduce-scatter.13
where the time goes:
time: 1500 us
  waiting for transfers between devices  1100 us (73%)
  matrix products  147 us (10%)
  local copies, waits for them, and re-layouts  117 us (8%)
  blocking collectives  82.7 us (6%)
  other arithmetic  25.5 us (2%)
  between operations  17 us (1%)
    reduce_scatter x3, waiting for transfers between devices, backward(): lax.psum_scatter(terms, 'ctx', scatter_dimension=1, tiled=True)  183 us
    all_gather x3, waiting for transfers between devices, body(): lax.all_gather(forward_values_own, 'ctx', axis=1, tiled=True)  170 us
    reduce_scatter x1, waiting for transfers between devices, body(): lax.psum_scatter(grads[3], ('seq', 'ctx'), scatter_dimension=0, tiled=True)  142 us
    reduce_scatter x1, waiting for transfers between devices, body(): lax.psum_scatter(grads[2], ('seq', 'ctx'), scatter_dimension=0, tiled=True)  141 us
    all_gather x3, waiting for transfers between devices, body(): lax.all_gather(forward_keys_own, 'ctx', axis=1, tiled=True)  137 us
    reduce_scatter x1, waiting for transfers between devices, body(): lax.psum_scatter(grads[0], ('seq', 'ctx'), scatter_dimension=0, tiled=True)  125 us
    unnamed x2, blocking collectives  82.7 us
    all_gather x1, waiting for transfers between devices, fetch(): lax.all_gather(down_weight, ('seq', 'ctx'), axis=0, tiled=True)  60.9 us
  transfers between devices with their start and end apart: 17, of which 16 were waited for; matrix products, arithmetic and copies ran while one was open for 15% of the time, Pallas kernels for 0%

commit v1 on v0

--- a/solution.py
+++ b/solution.py
@@ -9,6 +9,35 @@
 EPS = 1e-05
 NEG = -1e30
 SCALE = 0.125
+
+
+def mark_vector(unit, out_dim):
+    top = jax.lax.axis_size("ctx")
+    value_now = jax.lax.axis_index("ctx")
+    oldest, current_block, seen_now = (top, value_now, unit.shape[out_dim])
+    shelf = tuple(((h, (h + 1) % oldest) for h in range(oldest)))
+    grid = tuple(((h, (h - 1) % oldest) for h in range(oldest)))
+    current_value = jnp.zeros(
+        (*unit.shape[:out_dim], oldest * seen_now, *unit.shape[out_dim + 1 :]), unit.dtype
+    )
+    current_value = lax.dynamic_update_slice_in_dim(
+        current_value, unit, current_block * seen_now, axis=out_dim
+    )
+    w_next = formed = unit
+    tile_out = oldest // 2
+    jj = 1
+    while jj < tile_out + 1:
+        w_next = jax.lax.ppermute(w_next, "ctx", shelf)
+        current_value = lax.dynamic_update_slice_in_dim(
+            current_value, w_next, (current_block - jj) % oldest * seen_now, axis=out_dim
+        )
+        if jj < oldest - tile_out:
+            formed = jax.lax.ppermute(formed, "ctx", grid)
+            current_value = lax.dynamic_update_slice_in_dim(
+                current_value, formed, (current_block + jj) % oldest * seen_now, axis=out_dim
+            )
+        jj = jj + 1
+    return current_value
 
 
 def crms(inputs, gains):
@@ -260,7 +289,7 @@
             initial,
             (
                 lax.all_gather(forward_keys_own, "ctx", axis=1, tiled=True),
-                lax.all_gather(forward_values_own, "ctx", axis=1, tiled=True),
+                mark_vector(forward_values_own, 1),
             ),
         )
         heads_out = accum / denom[..., None]

time: 1500 us -> 1520 us (1.013)
  waiting for transfers between devices: 1100 us -> 980 us
  local copies, waits for them, and re-layouts: 117 us -> 214 us
  starting transfers between devices: 1.54 us -> 32.2 us
    dynamic_update_slice x0 -> x24, local copies, waits for them, and re-layouts: none -> 98.3 us  [the longest x12 53.5 us: mark_vector(): lax.dynamic_update_slice_in_dim(current_value, w_next, (current_block - j...]
    all_gather x3, waiting for transfers between devices: 137 us -> 41.5 us  [body(): lax.all_gather(forward_keys_own, 'ctx', axis=1, tiled=True)]
    all_gather x3, waiting for transfers between devices: 170 us -> 77.7 us  [backward(): lax.all_gather(values_own, 'ctx', axis=1, tiled=True)]
    ppermute x0 -> x21, waiting for transfers between devices: none -> 62.8 us  [the longest x9 41.7 us: mark_vector(): formed = jax.lax.ppermute(formed, 'ctx', grid)]
    all_gather x1, waiting for transfers between devices: 44.4 us -> 0.01 us  [fetch(): lax.all_gather(out_weight, ('seq', 'ctx'), axis=0, tiled=True)]
    reduce_scatter x3, waiting for transfers between devices: 183 us -> 221 us  [backward(): lax.psum_scatter(terms, 'ctx', scatter_dimension=1, tiled=True)]
    ppermute x0 -> x21, starting transfers between devices: none -> 31 us  [the longest x9 21.9 us: mark_vector(): formed = jax.lax.ppermute(formed, 'ctx', grid)]
    unnamed x344 -> x397, local copies, waits for them, and re-layouts: 19.2 us -> 32.9 us
  transfers between devices with their start and end apart: 17 -> 38, of which waited for: 16 -> 28; matrix products, arithmetic and copies ran while one was open for 15% -> 24% of each run, Pallas kernels for 0% -> 0%
where the time goes in v1:
time: 1520 us; the launch traced here: 1500 us
  waiting for transfers between devices  980 us (64%)
  local copies, waits for them, and re-layouts  214 us (14%)
  matrix products  143 us (9%)
  blocking collectives  82.8 us (5%)
  starting transfers between devices  32.2 us (2%)
  other arithmetic  28.4 us (2%)
  between operations  17.3 us (1%)
    reduce_scatter x3, waiting for transfers between devices, backward(): lax.psum_scatter(terms, 'ctx', scatter_dimension=1, tiled=True)  221 us
    reduce_scatter x1, waiting for transfers between devices, body(): lax.psum_scatter(grads[3], ('seq', 'ctx'), scatter_dimension=0, tiled=True)  142 us
    reduce_scatter x1, waiting for transfers between devices, body(): lax.psum_scatter(grads[2], ('seq', 'ctx'), scatter_dimension=0, tiled=True)  141 us
    reduce_scatter x1, waiting for transfers between devices, body(): lax.psum_scatter(grads[0], ('seq', 'ctx'), scatter_dimension=0, tiled=True)  125 us
    unnamed x2, blocking collectives  82.8 us
    all_gather x3, waiting for transfers between devices, backward(): lax.all_gather(values_own, 'ctx', axis=1, tiled=True)  77.7 us
    all_gather x1, waiting for transfers between devices, fetch(): lax.all_gather(down_weight, ('seq', 'ctx'), axis=0, tiled=True)  61.1 us
    all_gather x1, waiting for transfers between devices, fetch(): lax.all_gather(up_weight, ('seq', 'ctx'), axis=0, tiled=True)  60.6 us
  transfers between devices with their start and end apart: 38, of which 28 were waited for; matrix products, arithmetic and copies ran while one was open for 24% of the time, Pallas kernels for 0%

profile of v1, /device:TPU:0, one launch (start us, length us, event | category | flops | bytes accessed | tf_op | source)
XLA Modules:
  0.0 1503.4 jit_solution(18432916350200224412)
XLA Ops:
  10.4 42.3 %all-reduce.5 = (bf16[768]{0:T(1024)(128)(2,1)S(1)}, bf16[768]{0:T(1024)(128)(2,1)}) all-reduce(bf16[768]{0:T(1024)(128)(2,1)S(1)} %dynamic-update-slice, bf16[768]{0:T(1024)(128)(2,1)S(1)} %dynamic-update-slice.1), channel_id=1, replica_groups=mesh['seq'=4,'ctx'=8] {'seq','ctx'}, use_global_device_ids=true, to_apply=%add | all-reduce | flops 1536 | bytes 6144
  53.6 20.3 %all-gather.11.cloned.1.call-done = bf16[768,2304]{1,0:T(8,128)(2,1)} async-done(((bf16[24,2304]{1,0:T(8,128)(2,1)}), bf16[768,2304]{1,0:T(8,128)(2,1)}) %all-gather.11.cloned.1.call-update) | async-done | bytes 3538960 | tf_op jit(solution)/shard_map/all_gather | solution.py:132
  120.9 10.2 collective-permute-done.15
  131.1 6.0 collective-permute-done.7
  137.1 7.4 collective-permute-done.8
  149.8 7.3 collective-permute-done.1
  162.4 7.3 collective-permute-done.17
  187.3 4.8 collective-permute-done.19
  226.6 4.9 dynamic_update_slice.116
  276.4 4.8 dynamic_update_slice.120
  281.2 12.7 dynamic_update_slice.111
  307.1 5.0 copy.297
  333.1 41.4 %all-gather.13.cloned.1.call-done = bf16[1,768,12,64]{3,2,0,1:T(8,128)(2,1)} async-done(((bf16[1,96,12,64]{3,2,0,1:T(8,128)(2,1)}), bf16[1,768,12,64]{3,2,0,1:T(8,128)(2,1)}) %all-gather.13.cloned.1.call-update) | async-done | bytes 1179664 | tf_op jit(solution)/shard_map/all_gather | solution.py:291
  374.5 5.0 copy.279
  385.6 50.0 %all-gather.29.cloned.1.call-done = bf16[1,768,12,64]{3,2,0,1:T(8,128)(2,1)} async-done(((bf16[1,96,12,64]{3,2,0,1:T(8,128)(2,1)}), bf16[1,768,12,64]{3,2,0,1:T(8,128)(2,1)}) %all-gather.29.cloned.1.call-update) | async-done | bytes 1179664 | tf_op jit(solution)/shard_map/all_gather | solution.py:181
  440.3 60.6 %all-gather.17.cloned.1.call-done = bf16[768,3072]{1,0:T(8,128)(2,1)} async-done(((bf16[24,3072]{1,0:T(8,128)(2,1)}), bf16[768,3072]{1,0:T(8,128)(2,1)}) %all-gather.17.cloned.1.call-update) | async-done | bytes 4718608 | tf_op jit(solution)/shard_map/all_gather | solution.py:134
  505.2 61.1 %all-gather.19.cloned.1.call-done = bf16[3072,767]{1,0:T(8,128)(2,1)} async-done(((bf16[96,767]{1,0:T(8,128)(2,1)}), bf16[3072,767]{1,0:T(8,128)(2,1)}) %all-gather.19.cloned.1.call-update) | async-done | bytes 4712464 | tf_op jit(solution)/shard_map/all_gather | solution.py:135
  586.3 31.5 %while.11 = (s32[]{:T(128)}, f32[1,96,12,64]{1,3,2,0:T(8,128)}, f32[3,1,256,12,128]{4,2,0,3,1:T(8,128)}, s32[3]{0:T(128)S(1)}, bf16[1,768,12,64]{1,3,2,0:T(8,128...) while((s32[]{:T(128)}, f32[1,96,12,64]{1,3,2,0:T(8,128)}, ...), condition=%wide.region_33.34_spmd.clone, body=%wide.region_32.33_spmd.clone.sunk | while | flops 191693152 | bytes 18910308 | solution.py:204
  619.2 8.6 all-gather.27.cloned.1.call-done
  638.2 31.5 %while.10 = (s32[]{:T(128)}, f32[1,96,12,64]{1,3,2,0:T(8,128)}, f32[3,1,256,12,128]{4,2,0,3,1:T(8,128)}, s32[3]{0:T(128)S(1)}, bf16[1,768,12,64]{1,3,2,0:T(8,128...) while((s32[]{:T(128)}, f32[1,96,12,64]{1,3,2,0:T(8,128)}, ...), condition=%wide.region_27.28_spmd.clone, body=%wide.region_26.27_spmd.clone.sunk | while | flops 191693152 | bytes 18895424 | solution.py:204
  669.9 19.0 %all-gather.25.cloned.1.call-done = bf16[1,768,12,64]{3,2,0,1:T(8,128)(2,1)} async-done(((bf16[1,96,12,64]{3,2,0,1:T(8,128)(2,1)}), bf16[1,768,12,64]{3,2,0,1:T(8,128)(2,1)}) %all-gather.25.cloned.1.call-update) | async-done | bytes 1179664 | tf_op jit(solution)/shard_map/all_gather | solution.py:181
  697.7 26.4 %while.9 = (s32[]{:T(128)}, f32[1,96,12,64]{1,3,2,0:T(8,128)}, f32[3,1,256,12,128]{4,2,0,3,1:T(8,128)}, s32[3]{0:T(128)S(1)}, bf16[1,768,12,64]{1,3,2,0:T(8,128)...) while((s32[]{:T(128)}, f32[1,96,12,64]{1,3,2,0:T(8,128)}, ...), condition=%wide.region_21.22_spmd.clone, body=%wide.region_20.21_spmd.clone.sunk | while | flops 191693152 | bytes 18846272 | solution.py:204
  733.0 5.3 add_add_fusion
  743.4 5.0 add_add_fusion.1
  753.8 32.7 %reduce-scatter.12.cloned.1.call-done = f32[1,96,12,128]{3,1,2,0:T(8,128)} async-done(((f32[1,768,12,128]{3,1,2,0:T(8,128)}), f32[1,96,12,128]{3,1,2,0:T(8,128)}) %reduce-scatter.12.cloned.1.call-update) | async-done | bytes 589840 | tf_op jit(solution)/shard_map/reduce_scatter | solution.py:206
  791.1 94.0 %reduce-scatter.10.cloned.1.call-done = f32[1,96,12,128]{3,1,2,0:T(8,128)} async-done(((f32[1,768,12,128]{3,1,2,0:T(8,128)}), f32[1,96,12,128]{3,1,2,0:T(8,128)}) %reduce-scatter.10.cloned.1.call-update) | async-done | bytes 589840 | tf_op jit(solution)/shard_map/reduce_scatter | solution.py:206
  889.6 94.1 %reduce-scatter.8.cloned.1.call-done = f32[1,96,12,128]{3,1,2,0:T(8,128)} async-done(((f32[1,768,12,128]{3,1,2,0:T(8,128)}), f32[1,96,12,128]{3,1,2,0:T(8,128)}) %reduce-scatter.8.cloned.1.call-update) | async-done | bytes 589840 | tf_op jit(solution)/shard_map/reduce_scatter | solution.py:206
  1022.7 40.6 %all-reduce.4 = (f32[768]{0:T(1024)S(1)}, f32[768]{0:T(1024)S(1)}) all-reduce(f32[768]{0:T(1024)S(1)} %add_add_fusion.11, f32[768]{0:T(1024)S(1)} %copy-done.125), channel_id=21, replica_groups=mesh['seq'=4,'ctx'=8] {'seq','ctx'}, use_global_device_ids=true, to_apply=%region_49.50.clone | all-reduce | flops 1536 | bytes 12288
  1064.5 23.9 %reduce-scatter.16.cloned.1.call-done = f32[24,767]{1,0:T(8,128)} async-done(((f32[768,767]{1,0:T(8,128)}), f32[24,767]{1,0:T(8,128)}) %reduce-scatter.16.cloned.1.call-update) | async-done | bytes 73648 | tf_op jit(solution)/shard_map/reduce_scatter | solution.py:330
  1088.4 142.0 %reduce-scatter.20.cloned.1.call-done = f32[96,767]{1,0:T(8,128)} async-done(((f32[3072,767]{1,0:T(8,128)}), f32[96,767]{1,0:T(8,128)}) %reduce-scatter.20.cloned.1.call-update) | async-done | bytes 294544 | tf_op jit(solution)/shard_map/reduce_scatter | solution.py:332
  1230.4 140.9 %reduce-scatter.18.cloned.1.call-done = f32[24,3072]{1,0:T(8,128)} async-done(((f32[768,3072]{1,0:T(8,128)}), f32[24,3072]{1,0:T(8,128)}) %reduce-scatter.18.cloned.1.call-update) | async-done | bytes 294928 | tf_op jit(solution)/shard_map/reduce_scatter | solution.py:331
  1371.2 125.1 %reduce-scatter.14.cloned.1.call-done = f32[24,2304]{1,0:T(8,128)} async-done(((f32[768,2304]{1,0:T(8,128)}), f32[24,2304]{1,0:T(8,128)}) %reduce-scatter.14.cloned.1.call-update) | async-done | bytes 221200 | tf_op jit(solution)/shard_map/reduce_scatter | solution.py:329
  (825 shorter events, 397.0 us)
Async XLA Ops:
  7.2 66.7 %all-gather.11.cloned.1.call-start = ((), (), s32[]{:S(2)}) async-start(), calls=%async_computation.7 | async-start | bytes 3649536 | tf_op jit(solution)/shard_map/all_gather | solution.py:132
  7.9 299.2 %all-gather.23.cloned.1.call-start = ((), (), s32[]{:S(2)}) async-start(), calls=%async_computation.13 | async-start | bytes 3538944 | tf_op jit(solution)/shard_map/all_gather | solution.py:291
  81.7 236.3 %all-gather.15.cloned.1.call-start = ((), (), s32[]{:S(2)}) async-start(), calls=%async_computation.9 | async-start | bytes 1216512 | tf_op jit(solution)/shard_map/all_gather | solution.py:133
  82.5 238.8 %all-gather.21.cloned.1.call-start = ((), (), s32[]{:S(2)}) async-start(), calls=%async_computation.12 | async-start | bytes 3538944 | tf_op jit(solution)/shard_map/all_gather | solution.py:291
  93.2 281.3 %all-gather.13.cloned.1.call-start = ((), (), s32[]{:S(2)}) async-start(), calls=%async_computation.8 | async-start | bytes 3538944 | tf_op jit(solution)/shard_map/all_gather | solution.py:291
  100.8 334.8 %all-gather.29.cloned.1.call-start = ((), (), s32[]{:S(2)}) async-start(), calls=%async_computation.18 | async-start | bytes 3538944 | tf_op jit(solution)/shard_map/all_gather | solution.py:181
  102.2 398.7 %all-gather.17.cloned.1.call-start = ((), (), s32[]{:S(2)}) async-start(), calls=%async_computation.10 | async-start | bytes 4866048 | tf_op jit(solution)/shard_map/all_gather | solution.py:134
  102.9 463.4 %all-gather.19.cloned.1.call-start = ((), (), s32[]{:S(2)}) async-start(), calls=%async_computation.11 | async-start | bytes 4866048 | tf_op jit(solution)/shard_map/all_gather | solution.py:135
  103.7 524.1 %all-gather.27.cloned.1.call-start = ((), (), s32[]{:S(2)}) async-start(), calls=%async_computation.16 | async-start | bytes 3538944 | tf_op jit(solution)/shard_map/all_gather | solution.py:181
  105.0 583.9 %all-gather.25.cloned.1.call-start = ((), (), s32[]{:S(2)}) async-start(), calls=%async_computation.14 | async-start | bytes 3538944 | tf_op jit(solution)/shard_map/all_gather | solution.py:181
  107.4 23.7 %collective-permute-start.15 = (bf16[1,96,12,64]{1,3,2,0:T(8,128)(2,1)S(1)}, bf16[1,96,12,64]{1,3,2,0:T(8,128)(2,1)S(1)}, u32[]{:S(2)}, u32[]{:S(2)}) collective-permute-start(bf16[1,96,12,64]{1,3,2,0:T(8,128)(2,1)S(1)} %bitcast.715), channel_id=1, source_target_pairs={{0,7},{1,0},{2,1},{3,2},{4,3},{5,4},{6,5},{7,6},{8,15},{9,8},{10,9... | collective-permute-start | bytes 442376 | tf_op jit(solution)/shard_map/ppermute | solution.py:35
  110.6 26.4 %collective-permute-start.7 = (bf16[1,96,12,64]{1,3,2,0:T(8,128)(2,1)S(1)}, bf16[1,96,12,64]{1,3,2,0:T(8,128)(2,1)S(1)}, u32[]{:S(2)}, u32[]{:S(2)}) collective-permute-start(bf16[1,96,12,64]{1,3,2,0:T(8,128)(2,1)S(1)} %bitcast.718), channel_id=1, source_target_pairs={{0,1},{1,2},{2,3},{3,4},{4,5},{5,6},{6,7},{7,0},{8,9},{9,10},{10,1... | collective-permute-start | bytes 442376 | tf_op jit(solution)/shard_map/ppermute | solution.py:30
  110.6 33.9 %collective-permute-start.8 = (bf16[1,96,12,64]{1,3,2,0:T(8,128)(2,1)S(1)}, bf16[1,96,12,64]{1,3,2,0:T(8,128)(2,1)S(1)}, u32[]{:S(2)}, u32[]{:S(2)}) collective-permute-start(bf16[1,96,12,64]{1,3,2,0:T(8,128)(2,1)S(1)} %bitcast.719), channel_id=1, source_target_pairs={{0,7},{1,0},{2,1},{3,2},{4,3},{5,4},{6,5},{7,6},{8,15},{9,8},{10,9... | collective-permute-start | bytes 442376 | tf_op jit(solution)/shard_map/ppermute | solution.py:35
  115.5 32.5 %collective-permute-start = (bf16[1,96,12,64]{1,3,2,0:T(8,128)(2,1)S(1)}, bf16[1,96,12,64]{1,3,2,0:T(8,128)(2,1)S(1)}, u32[]{:S(2)}, u32[]{:S(2)}) collective-permute-start(bf16[1,96,12,64]{1,3,2,0:T(8,128)(2,1)S(1)} %bitcast.721), channel_id=1, source_target_pairs={{0,1},{1,2},{2,3},{3,4},{4,5},{5,6},{6,7},{7,0},{8,9},{9,10},{10,1... | collective-permute-start | bytes 442376 | tf_op jit(solution)/shard_map/ppermute | solution.py:30
  117.8 39.3 %collective-permute-start.1 = (bf16[1,96,12,64]{1,3,2,0:T(8,128)(2,1)S(1)}, bf16[1,96,12,64]{1,3,2,0:T(8,128)(2,1)S(1)}, u32[]{:S(2)}, u32[]{:S(2)}) collective-permute-start(bf16[1,96,12,64]{1,3,2,0:T(8,128)(2,1)S(1)} %bitcast.722), channel_id=1, source_target_pairs={{0,7},{1,0},{2,1},{3,2},{4,3},{5,4},{6,5},{7,6},{8,15},{9,8},{10,9... | collective-permute-start | bytes 442376 | tf_op jit(solution)/shard_map/ppermute | solution.py:35
  131.1 29.5 %collective-permute-start.16 = (bf16[1,96,12,64]{1,3,2,0:T(8,128)(2,1)S(1)}, bf16[1,96,12,64]{1,3,2,0:T(8,128)(2,1)S(1)}, u32[]{:S(2)}, u32[]{:S(2)}) collective-permute-start(bf16[1,96,12,64]{1,3,2,0:T(8,128)(2,1)S(1)} %collective-permute-done.14), channel_id=1, source_target_pairs={{0,1},{1,2},{2,3},{3,4},{4,5},{5,6},{6,7},{7,0},{8,9},{9,10},{10,1... | collective-permute-start | bytes 442376 | tf_op jit(solution)/shard_map/ppermute | solution.py:30
  137.1 32.7 %collective-permute-start.17 = (bf16[1,96,12,64]{1,3,2,0:T(8,128)(2,1)S(1)}, bf16[1,96,12,64]{1,3,2,0:T(8,128)(2,1)S(1)}, u32[]{:S(2)}, u32[]{:S(2)}) collective-permute-start(bf16[1,96,12,64]{1,3,2,0:T(8,128)(2,1)S(1)} %collective-permute-done.15), channel_id=1, source_target_pairs={{0,7},{1,0},{2,1},{3,2},{4,3},{5,4},{6,5},{7,6},{8,15},{9,8},{10,9... | collective-permute-start | bytes 442376 | tf_op jit(solution)/shard_map/ppermute | solution.py:35
  144.5 26.4 %collective-permute-start.9 = (bf16[1,96,12,64]{1,3,2,0:T(8,128)(2,1)S(1)}, bf16[1,96,12,64]{1,3,2,0:T(8,128)(2,1)S(1)}, u32[]{:S(2)}, u32[]{:S(2)}) collective-permute-start(bf16[1,96,12,64]{1,3,2,0:T(8,128)(2,1)S(1)} %collective-permute-done.7), channel_id=1, source_target_pairs={{0,1},{1,2},{2,3},{3,4},{4,5},{5,6},{6,7},{7,0},{8,9},{9,10},{10,1... | collective-permute-start | bytes 442376 | tf_op jit(solution)/shard_map/ppermute | solution.py:30
  148.0 28.2 %collective-permute-start.10 = (bf16[1,96,12,64]{1,3,2,0:T(8,128)(2,1)S(1)}, bf16[1,96,12,64]{1,3,2,0:T(8,128)(2,1)}, u32[]{:S(2)}, u32[]{:S(2)}) collective-permute-start(bf16[1,96,12,64]{1,3,2,0:T(8,128)(2,1)S(1)} %collective-permute-done.8), channel_id=1, source_target_pairs={{0,7},{1,0},{2,1},{3,2},{4,3},{5,4},{6,5},{7,6},{8,15},{9,8},{10,9... | collective-permute-start | bytes 442376 | tf_op jit(solution)/shard_map/ppermute | solution.py:35
  176.2 24.1 %collective-permute-start.4 = (bf16[1,96,12,64]{1,3,2,0:T(8,128)(2,1)S(1)}, bf16[1,96,12,64]{1,3,2,0:T(8,128)(2,1)}, u32[]{:S(2)}, u32[]{:S(2)}) collective-permute-start(bf16[1,96,12,64]{1,3,2,0:T(8,128)(2,1)S(1)} %collective-permute-done.2), channel_id=1, source_target_pairs={{0,1},{1,2},{2,3},{3,4},{4,5},{5,6},{6,7},{7,0},{8,9},{9,10},{10,1... | collective-permute-start | bytes 442376 | tf_op jit(solution)/shard_map/ppermute | solution.py:30
  183.4 92.9 %collective-permute-start.12 = (bf16[1,96,12,64]{1,3,2,0:T(8,128)(2,1)}, bf16[1,96,12,64]{1,3,2,0:T(8,128)(2,1)}, u32[]{:S(2)}, u32[]{:S(2)}) collective-permute-start(bf16[1,96,12,64]{1,3,2,0:T(8,128)(2,1)} %collective-permute-done.10), channel_id=1, source_target_pairs={{0,7},{1,0},{2,1},{3,2},{4,3},{5,4},{6,5},{7,6},{8,15},{9,8},{10,9... | collective-permute-start | bytes 442376 | tf_op jit(solution)/shard_map/ppermute | solution.py:35
  183.5 110.5 %collective-permute-start.5 = (bf16[1,96,12,64]{1,3,2,0:T(8,128)(2,1)}, bf16[1,96,12,64]{1,3,2,0:T(8,128)(2,1)}, u32[]{:S(2)}, u32[]{:S(2)}) collective-permute-start(bf16[1,96,12,64]{1,3,2,0:T(8,128)(2,1)} %collective-permute-done.3), channel_id=1, source_target_pairs={{0,7},{1,0},{2,1},{3,2},{4,3},{5,4},{6,5},{7,6},{8,15},{9,8},{10,9... | collective-permute-start | bytes 442376 | tf_op jit(solution)/shard_map/ppermute | solution.py:35
  192.1 106.1 %collective-permute-start.20 = (bf16[1,96,12,64]{1,3,2,0:T(8,128)(2,1)}, bf16[1,96,12,64]{1,3,2,0:T(8,128)(2,1)}, u32[]{:S(2)}, u32[]{:S(2)}) collective-permute-start(bf16[1,96,12,64]{1,3,2,0:T(8,128)(2,1)} %collective-permute-done.18), channel_id=1, source_target_pairs={{0,1},{1,2},{2,3},{3,4},{4,5},{5,6},{6,7},{7,0},{8,9},{9,10},{10,1... | collective-permute-start | bytes 442376 | tf_op jit(solution)/shard_map/ppermute | solution.py:30
  194.0 106.8 %collective-permute-start.13 = (bf16[1,96,12,64]{1,3,2,0:T(8,128)(2,1)}, bf16[1,96,12,64]{1,3,2,0:T(8,128)(2,1)}, u32[]{:S(2)}, u32[]{:S(2)}) collective-permute-start(bf16[1,96,12,64]{1,3,2,0:T(8,128)(2,1)} %collective-permute-done.11), channel_id=1, source_target_pairs={{0,1},{1,2},{2,3},{3,4},{4,5},{5,6},{6,7},{7,0},{8,9},{9,10},{10,1... | collective-permute-start | bytes 442376 | tf_op jit(solution)/shard_map/ppermute | solution.py:30
  200.4 104.1 %collective-permute-start.6 = (bf16[1,96,12,64]{1,3,2,0:T(8,128)(2,1)}, bf16[1,96,12,64]{1,3,2,0:T(8,128)(2,1)}, u32[]{:S(2)}, u32[]{:S(2)}) collective-permute-start(bf16[1,96,12,64]{1,3,2,0:T(8,128)(2,1)} %collective-permute-done.4), channel_id=1, source_target_pairs={{0,1},{1,2},{2,3},{3,4},{4,5},{5,6},{6,7},{7,0},{8,9},{9,10},{10,1... | collective-permute-start | bytes 442376 | tf_op jit(solution)/shard_map/ppermute | solution.py:30
  215.3 571.2 %reduce-scatter.12.cloned.1.call-start = ((), (), s32[]{:S(2)}) async-start(), calls=%async_computation.19 | async-start | bytes 5308416 | tf_op jit(solution)/shard_map/reduce_scatter | solution.py:206
  617.9 267.2 %reduce-scatter.10.cloned.1.call-start = ((), (), s32[]{:S(2)}) async-start(), calls=%async_computation.17 | async-start | bytes 5308416 | tf_op jit(solution)/shard_map/reduce_scatter | solution.py:206
  669.8 313.9 %reduce-scatter.8.cloned.1.call-start = ((), (), s32[]{:S(2)}) async-start(), calls=%async_computation.15 | async-start | bytes 5308416 | tf_op jit(solution)/shard_map/reduce_scatter | solution.py:206
  724.1 364.3 %reduce-scatter.16.cloned.1.call-start = ((), (), s32[]{:S(2)}) async-start(), calls=%async_computation.21 | async-start | bytes 2433024 | tf_op jit(solution)/shard_map/reduce_scatter | solution.py:330
  728.6 501.8 %reduce-scatter.20.cloned.1.call-start = ((), (), s32[]{:S(2)}) async-start(), calls=%async_computation.23 | async-start | bytes 9732096 | tf_op jit(solution)/shard_map/reduce_scatter | solution.py:332
  738.3 633.0 %reduce-scatter.18.cloned.1.call-start = ((), (), s32[]{:S(2)}) async-start(), calls=%async_computation.22 | async-start | bytes 9732096 | tf_op jit(solution)/shard_map/reduce_scatter | solution.py:331
  748.4 748.0 %reduce-scatter.14.cloned.1.call-start = ((), (), s32[]{:S(2)}) async-start(), calls=%async_computation.20 | async-start | bytes 7299072 | tf_op jit(solution)/shard_map/reduce_scatter | solution.py:329
  (226 other events, 3958.7 us)
Sparse Core Ops, SparseCore 0:
  10.9 62.9 all-gather.10
  81.8 102.3 all-gather.22
  187.2 63.9 all-gather.14
  253.8 59.4 all-gather.20
  315.4 59.1 all-gather.12
  376.6 59.0 all-gather.28
  438.6 62.2 all-gather.16
  503.8 62.4 all-gather.18
  568.5 59.2 all-gather.26
  629.8 59.0 all-gather.24
  692.6 93.8 reduce-scatter.11
  790.0 94.9 reduce-scatter.9
  888.7 95.0 reduce-scatter.7
  989.4 98.9 reduce-scatter.15
  1095.7 134.5 reduce-scatter.19
  1236.7 134.4 reduce-scatter.17
  1378.3 118.0 reduce-scatter.13
